TPU v7x, 256 devices: a whole 4x4x8 slice. The times are simulated.
256 devices in a mesh: row: 16 (over y, x_hi, core), col: 16 (over z, x_lo).
Axes of the slice: x: 4 (x_hi: 2, x_lo: 2; x = x_hi * 2 + x_lo), y: 4, z: 8, core: 2. Of those that a mesh axis runs over, the one named last changes fastest.
Arguments:
- density: bfloat16 [8192, 8192], P('row', 'col'), may hold values from -1 to 1
- pattern: int32 [32, 32], P('row', 'col'), may hold values from 0 to 1, as said below
Outputs:
- purified: bfloat16 [8192, 8192], P('row', 'col')
Inputs may be any that keep to these rules, and one draw needn't show every extreme that they name: pattern is symmetric with ones on its diagonal; no block row holds more than 12 ones, and some block row holds exactly 12.
All inputs are finite; a program needn't handle non-finite values.
Results may differ from a plain program's by a relative error of at most 0.0045.
Values may be sent and summed in bfloat16 or wider, within the bound.
A program may use at most 64 MiB of HBM per device.

v0:
```python
import jax
import jax.numpy as jnp
from jax import lax
from jax.sharding import PartitionSpec as P


def block_filter(matrix, pattern):
    rows_blocks = pattern.shape[0]
    cols_blocks = pattern.shape[1]
    size = matrix.shape[0] // rows_blocks
    shaped = matrix.reshape(rows_blocks, size, cols_blocks, size)
    keep = pattern.astype(matrix.dtype)[:, None, :, None]
    return (shaped * keep).reshape(matrix.shape)


def shards(density, pattern):
    filtered = block_filter(density, pattern)
    columns = lax.all_gather(filtered, "row", axis=0, tiled=True)
    panel = lax.all_gather(filtered, "col", axis=1, tiled=True)
    square = jnp.dot(panel, columns, preferred_element_type=jnp.float32)
    square = block_filter(square, pattern)
    square_low = square.astype(jnp.bfloat16)
    square_panel = lax.all_gather(square_low, "col", axis=1, tiled=True)
    cube = jnp.dot(square_panel, columns, preferred_element_type=jnp.float32)
    cube = block_filter(cube, pattern)
    return (3.0 * square - 2.0 * cube).astype(jnp.bfloat16)


def solution(mesh):
    return jax.shard_map(
        shards,
        mesh=mesh,
        in_specs=(P("row", "col"), P("row", "col")),
        out_specs=P("row", "col"),
        check_vma=False,
    )
```

profile of v0, /device:TPU:1, one launch (start us, length us, event | category | flops | bytes accessed | tf_op | source)
XLA Modules:
  0.0 487.4 jit_solution(12727660188539224904)
XLA Ops:
  6.5 0.0 all-gather.4.cloned.1.call-start
  6.5 0.8 fusion.3
  7.3 0.3 mul.41
  7.6 0.1 copy.3
  7.7 2.0 mul.43
  9.7 0.0 all-gather.4.cloned.1.call-update
  9.8 0.0 all-gather.6.cloned.1.call-start
  9.8 0.7 all-gather.6.cloned.1.call-update
  10.5 0.0 all-gather.8.cloned.1.call-start
  10.6 0.3 mul.44
  10.9 0.1 copy.4
  11.0 185.2 %all-gather.4.cloned.1.call-done = bf16[512,8192]{1,0:T(8,128)(2,1)} async-done(((bf16[512,512]{1,0:T(8,128)(2,1)}), bf16[512,8192]{1,0:T(8,128)(2,1)}) %all-gather.4.cloned.1.call-update) | async-done | bytes 8388624 | tf_op jit(solution)/shard_map/all_gather | solution.py:19
  196.2 82.4 %all-gather.6.cloned.1.call-done = bf16[8192,512]{1,0:T(8,128)(2,1)} async-done(((bf16[512,512]{1,0:T(8,128)(2,1)}), bf16[8192,512]{1,0:T(8,128)(2,1)}) %all-gather.6.cloned.1.call-update) | async-done | bytes 8388624 | tf_op jit(solution)/shard_map/all_gather | solution.py:18
  278.6 11.0 %fusion.4 = (bf16[512,512]{1,0:T(8,128)(2,1)}, f32[512,512]{1,0:T(8,128)S(1)}) fusion(f32[512,512]{1,0:T(8,128)S(1)} %bitcast.13, bf16[512,8192]{1,0:T(8,128)(2,1)} %all-gather.4.cloned.1.call-done, bf16[8192,512]{1,0:T(8,128)(2,1)} %all-gather.6.cloned.1.call-done), kind=kOutput, calls=%fused_computation.6 | convolution fusion | flops 4295491584 | bytes 19398656 | tf_op jit(solution)/shard_map/dot_general | solution.py:20
  289.7 0.0 all-gather.8.cloned.1.call-update
  289.7 180.0 %all-gather.8.cloned.1.call-done = bf16[512,8192]{1,0:T(8,128)(2,1)} async-done(((bf16[512,512]{1,0:T(8,128)(2,1)}), bf16[512,8192]{1,0:T(8,128)(2,1)}) %all-gather.8.cloned.1.call-update) | async-done | bytes 8388624 | tf_op jit(solution)/shard_map/all_gather | solution.py:23
  469.7 11.1 %fusion.2 = bf16[512,512]{1,0:T(8,128)(2,1)} fusion(f32[512,512]{1,0:T(8,128)S(1)} %bitcast.14, bf16[512,8192]{1,0:T(8,128)(2,1)} %all-gather.8.cloned.1.call-done, bf16[8192,512]{1,0:T(8,128)(2,1)} %all-gather.6.cloned.1.call-done, f32[512,512]{1,0:T(8,128)S(1)} %get-tuple-element.8), kind=kOutput, calls=%fused_computation.4 | convolution fusion | flops 4296278016 | bytes 19398656 | tf_op jit(solution)/shard_map/dot_general | solution.py:24
Async XLA Ops:
  6.5 189.7 %all-gather.4.cloned.1.call-start = ((), (), s32[]{:S(2)}) async-start(), calls=%async_computation | async-start | bytes 8912896 | tf_op jit(solution)/shard_map/all_gather | solution.py:19
  9.8 268.9 %all-gather.6.cloned.1.call-start = ((), (), s32[]{:S(2)}) async-start(), calls=%async_computation.1 | async-start | bytes 8912896 | tf_op jit(solution)/shard_map/all_gather | solution.py:18
  10.5 459.2 %all-gather.8.cloned.1.call-start = ((), (), s32[]{:S(2)}) async-start(), calls=%async_computation.2 | async-start | bytes 8912896 | tf_op jit(solution)/shard_map/all_gather | solution.py:23
Sparse Core Ops, SparseCore 0:
  9.9 186.2 all-gather.3
  198.9 79.6 all-gather.5
  289.8 179.8 all-gather.7
where the time goes:
time: 488 us; the launch traced here: 487 us
  waiting for transfers between devices  448 us (92%)
  matrix products  22.1 us (5%)
  between operations  13.1 us (3%)
    all_gather x1, waiting for transfers between devices, shards(): panel = lax.all_gather(filtered, 'col', axis=1, tiled=True)  185 us
    all_gather x1, waiting for transfers between devices, shards(): square_panel = lax.all_gather(square_low, 'col', axis=1, tiled=True)  180 us
    all_gather x1, waiting for transfers between devices, shards(): columns = lax.all_gather(filtered, 'row', axis=0, tiled=True)  82.4 us
    dot_general x1, matrix products, shards(): cube = jnp.dot(square_panel, columns, preferred_element_type=jnp.float32)  11.1 us
    dot_general x1, matrix products, shards(): square = jnp.dot(panel, columns, preferred_element_type=jnp.float32)  11 us
  transfers between devices with their start and end apart: 3, of which 3 were waited for; matrix products, arithmetic and copies ran while one was open for 0% of the time, Pallas kernels for 0%

commit v1 on v0

v1 whole, which is shorter than its diff:
```python
import functools

import jax
import jax.numpy as jnp
from jax import lax
from jax.experimental import pallas as pl
from jax.experimental.pallas import tpu as pltpu
from jax.sharding import PartitionSpec as P

MESH = pl.DeviceIdType.MESH
BF16 = jnp.bfloat16
F32 = jnp.float32
SIZE = 256
SLOTS = 12
NB = 32
GROUP = 16
PART = SIZE // GROUP


def place(x, y, z, core):
    return {"row": (y * 2 + lax.div(x, 2)) * 2 + core, "col": z * 2 + lax.rem(x, 2)}


def kernel(dens, patt, out, blocks, rr0, rr1, sr0, sr1, crecv, rp0, rp1, sp0, sp1, cp0, cp1, rhs0, rhs1, sf, sl, obuf, pmsg, prow, pcol, prow_s, pcol_s, nxt, idx, rank, a2a_send, row_recv, col_recv, pat_recv, pat_copy, s_send, s_recv, z_send, z_recv, mate_recv, c_send, c_recv, out_sem):
    rrecv, srecv, rpanel, spanel, cpanel, rhs = (rr0, rr1), (sr0, sr1), (rp0, rp1), (sp0, sp1), (cp0, cp1), (rhs0, rhs1)
    row, col = lax.axis_index("row"), lax.axis_index("col")
    y, xh, core = lax.div(row, 4), lax.rem(lax.div(row, 2), 2), lax.rem(row, 2)
    z, xl = lax.div(col, 2), lax.rem(col, 2)
    x = xh * 2 + xl
    pair = (y * 2 + xh) * 2
    part_z = z * 2 + core
    part_xy = y * 4 + x
    settled = xl == core

    def row_target(d):
        zz, cc = lax.rem(z + lax.div(d, 2), 8), lax.rem(core + d, 2)
        return zz * 2 + cc, {"row": pair + cc, "col": zz * 2 + core}

    def col_target(d):
        q = lax.rem(part_xy + d, GROUP)
        return q, {"row": lax.div(q, 2) * 2 + xl, "col": z * 2 + lax.rem(q, 2)}

    def mate_target(d):
        zz, cc = lax.rem(z + lax.div(d, 2), 8), lax.rem(core + d, 2)
        return zz * 2 + cc, {"row": pair + cc, "col": zz * 2 + xl}

    def z_side(s):
        return place(x, y, lax.rem(z + s + 8, 8), core)

    def xy_side(axis, s):
        if axis == 0:
            return place(lax.rem(x + s + 4, 4), y, z, core)
        return place(x, lax.rem(y + s + 4, 4), z, core)

    for i in range(2):
        for j in range(2):
            blocks[i, j] = dens[i, :, j * SIZE : (j + 1) * SIZE]

    barrier = pltpu.get_barrier_semaphore()

    def greet(d, _):
        @pl.when(jnp.logical_or(d != col, jnp.logical_not(settled)))
        def _():
            pl.semaphore_signal(barrier, 1, device_id={"row": part_xy, "col": d}, device_id_type=MESH)

        @pl.when(jnp.logical_or(d != row, jnp.logical_not(settled)))
        def _():
            pl.semaphore_signal(barrier, 1, device_id={"row": d, "col": part_z}, device_id_type=MESH)

        @pl.when(d != 0)
        def _():
            pl.semaphore_signal(barrier, 1, device_id=mate_target(d)[1], device_id_type=MESH)

        return 0

    lax.fori_loop(0, GROUP, greet, 0)
    for axis in range(2):
        for s in (1, -1):
            pl.semaphore_signal(barrier, 1, device_id=xy_side(axis, s), device_id_type=MESH)
    pl.semaphore_wait(barrier, jnp.where(settled, 30, 32) + 19)

    lane = lax.broadcasted_iota(jnp.int32, (1, 128), 1)
    entries = jnp.zeros((1, 128), jnp.int32)
    for i in range(2):
        for j in range(2):
            entries = jnp.where(lane == i * 2 + j, patt[i, j], entries)
    pmsg[...] = entries

    def send(src, dst, send_sem, recv_sem, device):
        pltpu.make_async_remote_copy(src_ref=src, dst_ref=dst, send_sem=send_sem, recv_sem=recv_sem, device_id=device, device_id_type=MESH).start()

    def deliver(d, src, dst, send_sem, recv_sem, device, always_self):
        here = d == 0 if always_self else jnp.logical_and(d == 0, settled)

        @pl.when(here)
        def _():
            pltpu.make_async_copy(src, dst, recv_sem).start()

        @pl.when(jnp.logical_not(here))
        def _():
            send(src, dst, send_sem, recv_sem, device)

    def wait_for(ref, sem):
        pltpu.make_async_copy(ref, ref, sem).wait()

    def send_patterns(d, _):
        _, device = row_target(d)
        deliver(d, pmsg, prow.at[col], a2a_send.at[2], pat_recv.at[0], device, False)
        _, device = col_target(d)
        deliver(d, pmsg, pcol.at[row], a2a_send.at[2], pat_recv.at[1], device, False)
        return 0

    lax.fori_loop(0, GROUP, send_patterns, 0)

    def send_rows(i):
        def body(n, _):
            d = lax.rem(n + 7, GROUP)
            s, device = row_target(d)
            deliver(d, blocks.at[i, :, pl.ds(pl.multiple_of(s * PART, PART), PART)], rrecv[i].at[pl.ds(2 * col, 2)], a2a_send.at[0], row_recv.at[i], device, False)
            return 0

        lax.fori_loop(0, GROUP, body, 0)

    def send_columns(n, _):
        d = lax.rem(n + 7, GROUP)
        q, device = col_target(d)
        deliver(d, dens.at[:, pl.ds(pl.multiple_of(q * PART, PART), PART)], crecv.at[pl.ds(2 * row, 2)], a2a_send.at[1], col_recv, device, False)
        return 0

    send_rows(0)
    lax.fori_loop(0, GROUP, send_columns, 0)
    send_rows(1)

    for received in (*rrecv, *srecv):
        received[NB] = jnp.zeros((PART, SIZE), BF16)
    crecv[NB] = jnp.zeros((PART, 2 * SIZE), BF16)
    for j in range(2):
        cpanel[j][:, SLOTS] = jnp.zeros((GROUP, PART, SIZE), BF16)

    wait_for(prow, pat_recv.at[0])
    wait_for(pcol, pat_recv.at[1])
    to_smem = [pltpu.make_async_copy(prow, prow_s, pat_copy.at[0]), pltpu.make_async_copy(pcol, pcol_s, pat_copy.at[1])]
    for c in to_smem:
        c.start()
    for c in to_smem:
        c.wait()

    def occupied(q, k):
        if q < 2:
            return prow_s[lax.div(k, 2), 0, q * 2 + lax.rem(k, 2)]
        return pcol_s[lax.div(k, 2), 0, lax.rem(k, 2) * 2 + (q - 2)]

    def backward(n, carry):
        k = NB - 1 - n
        later = []
        for q in range(4):
            nxt[q, k] = carry[q]
            later.append(carry[q] + occupied(q, k) * (k - carry[q]))
        return tuple(later)

    for q in range(4):
        nxt[q, NB] = NB
    first = lax.fori_loop(0, NB, backward, (jnp.int32(NB),) * 4)

    def forward(t, carry):
        later = []
        for q in range(4):
            idx[q, t] = carry[q]
            later.append(nxt[q, carry[q]])
        return tuple(later)

    lax.fori_loop(0, SLOTS, forward, first)

    def count(k, carry):
        later = []
        for j in range(2):
            is_on = occupied(2 + j, k)
            rank[j, k] = SLOTS + is_on * (carry[j] - SLOTS)
            later.append(carry[j] + is_on)
        return tuple(later)

    for j in range(2):
        rank[j, NB] = SLOTS
    lax.fori_loop(0, NB, count, (jnp.int32(0),) * 2)

    def unit(j, da, db):
        dx, dy = (da, db) if j == 0 else (db, da)
        return lax.rem(y + dy + 4, 4) * 4 + lax.rem(x + dx + 4, 4)

    order = {0: 0, -1: 1, 1: 2, 2: 3}

    def column_send(j, q, half, axis, s, n):
        slots = pl.ds(0, SLOTS) if half is None else pl.ds(half * (SLOTS // 2), SLOTS // 2)
        ref = cpanel[j].at[q, slots]
        send(ref, ref, c_send.at[j], c_recv.at[j, n], xy_side(axis, s))

    def column_wait(j, q, half, n):
        slots = pl.ds(0, SLOTS) if half is None else pl.ds(half * (SLOTS // 2), SLOTS // 2)
        wait_for(cpanel[j].at[q, slots], c_recv.at[j, n])

    def column_along(j, da):
        for way, s in enumerate((1, -1)):
            column_send(j, unit(j, da, 0), None, 1 - j, s, 4 + order[da] * 2 + way)

    def column_own(j):
        def body(t, _):
            cpanel[j][part_xy, t] = crecv[idx[2 + j, t], :, j * SIZE : (j + 1) * SIZE]
            return 0

        lax.fori_loop(0, SLOTS, body, 0)

    def column_first(j):
        for way, s in enumerate((1, -1)):
            column_send(j, unit(j, 0, 0), None, j, s, way)

    def column_near(j):
        for way, s in enumerate((1, -1)):
            column_wait(j, unit(j, -s, 0), None, way)
            column_send(j, unit(j, -s, 0), way, j, s, 2 + way)
        column_along(j, -1)
        column_along(j, 1)

    def column_far(j):
        for way in range(2):
            column_wait(j, unit(j, 2, 0), way, 2 + way)
        column_along(j, 2)

    def column_second(j, da):
        for way, s in enumerate((1, -1)):
            column_wait(j, unit(j, da, -s), None, 4 + order[da] * 2 + way)
            if (da in (0, -1)) == (s == 1):
                column_send(j, unit(j, da, -s), None, 1 - j, s, 12 + order[da])

    def column_last(j):
        for da in order:
            column_wait(j, unit(j, da, 2), None, 12 + order[da])

    def ring(i, stage):
        panel = (rpanel, spanel)[stage][i]
        sem = z_recv.at[stage, i]

        def ref(d, half=None):
            here = lax.rem(z + d + 8, 8) * 2 + core
            return panel.at[here] if half is None else panel.at[here, :, pl.ds(half * (SLOTS // 2 * SIZE), SLOTS // 2 * SIZE)]

        def to_mate(d):
            send(ref(d), ref(d), z_send.at[stage, i], mate_recv.at[stage, i], {"row": pair + 1 - core, "col": col})

        def compact(received):
            def body(t, _):
                panel[part_z, :, pl.ds(pl.multiple_of(t * SIZE, SIZE), SIZE)] = received[idx[i, t]]
                return 0

            lax.fori_loop(0, SLOTS, body, 0)

        def start():
            for way, s in enumerate((1, -1)):
                send(ref(0), ref(0), z_send.at[stage, i], sem.at[way, 0], z_side(s))
            to_mate(0)

        def hop(d):
            for way, s in enumerate((1, -1)):
                wait_for(ref(-s * d), sem.at[way, d - 1])
                half = None if d < 3 else way
                send(ref(-s * d, half), ref(-s * d, half), z_send.at[stage, i], sem.at[way, d], z_side(s))
            for s in (1, -1):
                to_mate(-s * d)

        def last():
            for way in range(2):
                wait_for(ref(4, way), sem.at[way, 3])
            to_mate(4)

        def finish():
            wait_for(panel.at[pl.ds(0, 8)], mate_recv.at[stage, i])

        return compact, start, hop, last, finish

    rows = [ring(0, 0), ring(1, 0)]

    def row_own(i):
        compact, start, _, _, _ = rows[i]
        wait_for(rrecv[i].at[pl.ds(0, NB)], row_recv.at[i])
        compact(rrecv[i])
        start()

    wait_for(crecv.at[pl.ds(0, NB)], col_recv)
    column_own(0)
    column_first(0)
    column_own(1)
    column_first(1)
    column_along(0, 0)
    column_along(1, 0)
    row_own(0)
    column_near(0)
    column_near(1)
    row_own(1)
    column_second(0, 0)
    column_second(1, 0)
    column_far(0)
    column_far(1)
    rows[0][2](1)
    column_second(0, -1)
    column_second(1, -1)
    rows[1][2](1)
    rows[0][2](2)
    column_second(0, 1)
    column_second(1, 1)
    rows[1][2](2)
    rows[0][2](3)
    column_second(0, 2)
    column_second(1, 2)
    rows[1][2](3)
    rows[0][3]()
    column_last(0)
    column_last(1)

    def gather_rhs(i):
        def body(t, _):
            k = idx[i, t]
            for j in range(2):
                block = cpanel[j][:, rank[j, k]]
                rhs[i][pl.ds(pl.multiple_of(t * SIZE, SIZE), SIZE), j * SIZE : (j + 1) * SIZE] = block.reshape(SIZE, SIZE)
            return 0

        lax.fori_loop(0, SLOTS, body, 0)

    def product(panel, i):
        whole = jnp.dot(panel[i][...].reshape(SIZE, SLOTS * SIZE), rhs[i][...], preferred_element_type=F32)
        keep = [prow_s[part_z, 0, i * 2 + j].astype(F32) for j in range(2)]
        return jnp.concatenate([whole[:, :SIZE] * keep[0], whole[:, SIZE:] * keep[1]], axis=1)

    def square(i):
        value = product(rpanel, i)
        sf[i] = value
        for j in range(2):
            sl[i, j] = value[:, j * SIZE : (j + 1) * SIZE].astype(BF16)

        def body(n, _):
            d = lax.rem(n + 7, GROUP)
            s, device = mate_target(d)
            deliver(d, sl.at[i, :, pl.ds(pl.multiple_of(s * PART, PART), PART)], srecv[i].at[pl.ds(2 * part_z, 2)], s_send.at[i], s_recv.at[i], device, True)
            return 0

        lax.fori_loop(0, GROUP, body, 0)

    gather_rhs(0)
    rows[0][4]()
    square(0)
    rows[1][3]()
    gather_rhs(1)
    rows[1][4]()
    square(1)

    squares = [ring(0, 1), ring(1, 1)]
    for i in range(2):
        wait_for(srecv[i].at[pl.ds(0, NB)], s_recv.at[i])
        squares[i][0](srecv[i])
        squares[i][1]()
    for d in (1, 2, 3):
        for i in range(2):
            squares[i][2](d)

    def cube(i):
        squares[i][3]()
        squares[i][4]()
        value = (3.0 * sf[i] - 2.0 * product(spanel, i)).astype(BF16)

        @pl.when(settled)
        def _():
            out[i] = value

        @pl.when(jnp.logical_not(settled))
        def _():
            obuf[i] = value
            send(obuf.at[i], out.at[i], out_sem.at[0, i], out_sem.at[1, i], {"row": pair + xl, "col": part_z})

    cube(0)
    cube(1)

    @pl.when(jnp.logical_not(settled))
    def _():
        for i in range(2):
            wait_for(out.at[i], out_sem.at[1, i])
            wait_for(obuf.at[i], out_sem.at[0, i])
        for i in range(2):
            wait_for(rrecv[i].at[pl.ds(0, 2)], a2a_send.at[0])
        wait_for(crecv.at[pl.ds(0, 2)], a2a_send.at[1])
        wait_for(prow.at[0], a2a_send.at[2])
        wait_for(pcol.at[0], a2a_send.at[2])

    for i in range(2):
        wait_for(rrecv[i].at[pl.ds(0, 30)], a2a_send.at[0])
    wait_for(crecv.at[pl.ds(0, 30)], a2a_send.at[1])
    wait_for(prow.at[pl.ds(1, 15)], a2a_send.at[2])
    wait_for(pcol.at[pl.ds(1, 15)], a2a_send.at[2])
    for i in range(2):
        wait_for(srecv[i].at[pl.ds(0, 30)], s_send.at[i])
        for stage in range(2):
            wait_for((rpanel, spanel)[stage][i].at[pl.ds(0, 15)], z_send.at[stage, i])
        wait_for(cpanel[i].at[pl.ds(0, 15), pl.ds(0, SLOTS)], c_send.at[i])


def shards(density, pattern):
    wide = SLOTS * SIZE
    vmem, smem, dma = pltpu.VMEM, pltpu.SMEM, pltpu.SemaphoreType.DMA
    received = vmem((NB + 1, PART, SIZE), BF16)
    panel = vmem((GROUP, PART, wide), BF16)
    purified = pl.pallas_call(
        kernel,
        out_shape=jax.ShapeDtypeStruct((2, SIZE, 2 * SIZE), BF16),
        in_specs=[pl.BlockSpec(memory_space=vmem), pl.BlockSpec(memory_space=smem)],
        out_specs=pl.BlockSpec(memory_space=vmem),
        scratch_shapes=[
            vmem((2, 2, SIZE, SIZE), BF16),
            received, received, received, received,
            vmem((NB + 1, PART, 2 * SIZE), BF16),
            panel, panel, panel, panel,
            vmem((GROUP, SLOTS + 1, PART, SIZE), BF16),
            vmem((GROUP, SLOTS + 1, PART, SIZE), BF16),
            vmem((wide, 2 * SIZE), BF16),
            vmem((wide, 2 * SIZE), BF16),
            vmem((2, SIZE, 2 * SIZE), F32),
            vmem((2, 2, SIZE, SIZE), BF16),
            vmem((2, SIZE, 2 * SIZE), BF16),
            vmem((1, 128), jnp.int32),
            vmem((GROUP, 1, 128), jnp.int32),
            vmem((GROUP, 1, 128), jnp.int32),
            smem((GROUP, 1, 128), jnp.int32),
            smem((GROUP, 1, 128), jnp.int32),
            smem((4, NB + 1), jnp.int32),
            smem((4, SLOTS), jnp.int32),
            smem((2, NB + 1), jnp.int32),
            dma((3,)), dma((2,)), dma, dma((2,)), dma((2,)),
            dma((2,)), dma((2,)), dma((2, 2)), dma((2, 2, 2, 4)), dma((2, 2)),
            dma((2,)), dma((2, 16)), dma((2, 2)),
        ],
        compiler_params=pltpu.CompilerParams(collective_id=0, has_side_effects=True, vmem_limit_bytes=48 * 2**20),
        name="purify",
    )(density.reshape(2, SIZE, 2 * SIZE), pattern)
    return purified.reshape(2 * SIZE, 2 * SIZE)


def solution(mesh):
    return jax.shard_map(
        shards,
        mesh=mesh,
        in_specs=(P("row", "col"), P("row", "col")),
        out_specs=P("row", "col"),
        check_vma=False,
    )
```

time: 488 us -> 94.9 us (0.19)
  waiting for transfers between devices: 448 us -> 0 us
  Pallas kernels: 0 us -> 92.3 us
  matrix products: 22.1 us -> 0 us
  between operations: 13.1 us -> 0.01 us
    all_gather x3 -> x0, waiting for transfers between devices: 448 us -> none  [the longest x1 185 us: shards(): panel = lax.all_gather(filtered, 'col', axis=1, tiled=True)]
    pallas_call x0 -> x1, Pallas kernels: none -> 92.3 us  [shards(): pl.pallas_call(kernel, out_shape=jax.ShapeDtypeStruct((2, SIZE, 2 * SIZE)...]
    dot_general x2 -> x0, matrix products: 22.1 us -> none  [the longest x1 11.1 us: shards(): cube = jnp.dot(square_panel, columns, preferred_element_type=jnp.float32)]
  transfers between devices with their start and end apart: 3 -> 0, of which waited for: 3 -> 0; matrix products, arithmetic and copies ran while one was open for 0% -> 0% of each run, Pallas kernels for 0% -> 0%
where the time goes in v1:
time: 94.9 us; the launch traced here: 94.8 us
  Pallas kernels  92.3 us (97%)
  local copies, waits for them, and re-layouts  2.52 us (3%)
    pallas_call x1, Pallas kernels, shards(): pl.pallas_call(kernel, out_shape=jax.ShapeDtypeStruct((2, SIZE, 2 * SIZE)...  92.3 us
    unnamed x5, local copies, waits for them, and re-layouts  2.52 us

profile of v1, /device:TPU:1, one launch (start us, length us, event | category | flops | bytes accessed | tf_op | source)
XLA Modules:
  0.0 94.8 jit_solution(1269063318222558648)
XLA Ops:
  0.0 0.0 copy-start.1
  0.0 0.7 copy-done.1
  0.7 0.0 copy-start
  0.7 1.0 %copy-done = bf16[512,512]{1,0:T(8,128)(2,1)S(1)} copy-done((bf16[512,512]{1,0:T(8,128)(2,1)S(1)}, bf16[512,512]{1,0:T(8,128)(2,1)}, u32[]{:S(2)}) %copy-start) | copy-done | bytes 524312
  1.7 92.3 %purify.1 = bf16[2,256,512]{2,1,0:T(8,128)(2,1)S(1)} custom-call(bf16[2,256,512]{2,1,0:T(8,128)(2,1)S(1)} %bitcast.3, s32[2,2]{1,0:T(2,128)S(1)} %copy-done.1), custom_call_target="tpu_custom_call" | custom-call | tf_op jit(solution)/shard_map/purify/pallas_call | solution.py:409
  94.0 0.8 copy.4
Async XLA Ops:
  0.0 0.7 copy-start.1
  0.7 1.0 %copy-start = (bf16[512,512]{1,0:T(8,128)(2,1)S(1)}, bf16[512,512]{1,0:T(8,128)(2,1)}, u32[]{:S(2)}) copy-start(bf16[512,512]{1,0:T(8,128)(2,1)} %param.2) | copy-start | bytes 1572868

commit v2 on v1

v2 whole, which is shorter than its diff:
```python
import functools

import jax
import jax.numpy as jnp
from jax import lax
from jax.experimental import pallas as pl
from jax.experimental.pallas import tpu as pltpu
from jax.sharding import PartitionSpec as P

MESH = pl.DeviceIdType.MESH
BF16 = jnp.bfloat16
F32 = jnp.float32
SIZE = 256
SLOTS = 12
HALF = SIZE // 2
NB = 32
GROUP = 16
PART = SIZE // GROUP


def place(x, y, z, core):
    return {"row": (y * 2 + lax.div(x, 2)) * 2 + core, "col": z * 2 + lax.rem(x, 2)}


def kernel(dens, patt_hbm, out, blocks, patt, rr0, rr1, rr2, rr3, sr0, sr1, sr2, sr3, crecv, panel, cp0, cp1, rhs, sf, cf, sl, obuf, pmsg, prow, pcol, prow_s, pcol_s, nxt, idx, rank, load_sem, a2a_send, row_recv, col_recv, pat_recv, pat_copy, s_send, s_recv, z_send, z_recv, mate_recv, c_send, c_recv, out_sem):
    rrecv, srecv, cpanel = (rr0, rr1, rr2, rr3), (sr0, sr1, sr2, sr3), (cp0, cp1)
    row, col = lax.axis_index("row"), lax.axis_index("col")
    y, xh, core = lax.div(row, 4), lax.rem(lax.div(row, 2), 2), lax.rem(row, 2)
    z, xl = lax.div(col, 2), lax.rem(col, 2)
    x = xh * 2 + xl
    pair = (y * 2 + xh) * 2
    part_z = z * 2 + core
    part_xy = y * 4 + x
    settled = xl == core

    def row_target(d):
        zz, cc = lax.rem(z + lax.div(d, 2), 8), lax.rem(core + d, 2)
        return zz * 2 + cc, {"row": pair + cc, "col": zz * 2 + core}

    def col_target(d):
        q = lax.rem(part_xy + d, GROUP)
        return q, {"row": lax.div(q, 2) * 2 + xl, "col": z * 2 + lax.rem(q, 2)}

    def mate_target(d):
        zz, cc = lax.rem(z + lax.div(d, 2), 8), lax.rem(core + d, 2)
        return zz * 2 + cc, {"row": pair + cc, "col": zz * 2 + xl}

    def z_side(s):
        return place(x, y, lax.rem(z + s + 8, 8), core)

    def xy_side(axis, s):
        if axis == 0:
            return place(lax.rem(x + s + 4, 4), y, z, core)
        return place(x, lax.rem(y + s + 4, 4), z, core)

    loads = [pltpu.make_async_copy(patt_hbm, patt, load_sem.at[0])]
    for i in range(2):
        for j in range(2):
            loads.append(pltpu.make_async_copy(dens.at[i, :, pl.ds(j * SIZE, SIZE)], blocks.at[i, j], load_sem.at[1 + 2 * i + j]))
    for load in loads:
        load.start()

    barrier = pltpu.get_barrier_semaphore()

    def greet(device):
        pl.semaphore_signal(barrier, 1, device_id=device, device_id_type=MESH)

    for d in range(GROUP):
        @pl.when(jnp.logical_or(d != col, jnp.logical_not(settled)))
        def _():
            greet({"row": part_xy, "col": d})

    for d in range(GROUP):
        @pl.when(jnp.logical_or(d != row, jnp.logical_not(settled)))
        def _():
            greet({"row": d, "col": part_z})

    for d in range(1, GROUP):
        greet(mate_target(d)[1])
    for axis in range(2):
        for s in (1, -1):
            greet(xy_side(axis, s))
    for load in loads:
        load.wait()
    pl.semaphore_wait(barrier, jnp.where(settled, 30, 32) + 19)

    lane = lax.broadcasted_iota(jnp.int32, (1, 128), 1)
    entries = jnp.zeros((1, 128), jnp.int32)
    for i in range(2):
        for j in range(2):
            entries = jnp.where(lane == i * 2 + j, patt[i, j], entries)
    pmsg[...] = entries

    def send(src, dst, send_sem, recv_sem, device):
        pltpu.make_async_remote_copy(src_ref=src, dst_ref=dst, send_sem=send_sem, recv_sem=recv_sem, device_id=device, device_id_type=MESH).start()

    def deliver(d, src, dst, send_sem, recv_sem, device, always_self):
        here = d == 0 if always_self else jnp.logical_and(d == 0, settled)

        @pl.when(here)
        def _():
            pltpu.make_async_copy(src, dst, recv_sem).start()

        @pl.when(jnp.logical_not(here))
        def _():
            send(src, dst, send_sem, recv_sem, device)

    def wait_for(ref, sem):
        pltpu.make_async_copy(ref, ref, sem).wait()

    def send_patterns(d, _):
        _, device = row_target(d)
        deliver(d, pmsg, prow.at[col], a2a_send.at[2], pat_recv.at[0], device, False)
        _, device = col_target(d)
        deliver(d, pmsg, pcol.at[row], a2a_send.at[2], pat_recv.at[1], device, False)
        return 0

    lax.fori_loop(0, GROUP, send_patterns, 0)

    def half(h):
        return pl.ds(h * HALF, HALF)

    def send_rows(c):
        def body(n, _):
            d = lax.rem(n + 7, GROUP)
            s, device = row_target(d)
            deliver(d, blocks.at[c // 2, :, pl.ds(pl.multiple_of(s * PART, PART), PART), half(c % 2)], rrecv[c].at[pl.ds(2 * col, 2)], a2a_send.at[0], row_recv.at[c], device, False)
            return 0

        lax.fori_loop(0, GROUP, body, 0)

    def send_columns(n, _):
        d = lax.rem(n + 7, GROUP)
        q, device = col_target(d)
        deliver(d, dens.at[:, pl.ds(pl.multiple_of(q * PART, PART), PART)], crecv.at[pl.ds(2 * row, 2)], a2a_send.at[1], col_recv, device, False)
        return 0

    send_rows(0)
    lax.fori_loop(0, GROUP, send_columns, 0)
    for c in range(1, 4):
        send_rows(c)

    for received in (*rrecv, *srecv):
        received[NB] = jnp.zeros((PART, HALF), BF16)
    crecv[NB] = jnp.zeros((PART, 2 * SIZE), BF16)
    for j in range(2):
        cpanel[j][:, SLOTS] = jnp.zeros((GROUP, PART, SIZE), BF16)

    wait_for(prow, pat_recv.at[0])
    wait_for(pcol, pat_recv.at[1])
    to_smem = [pltpu.make_async_copy(prow, prow_s, pat_copy.at[0]), pltpu.make_async_copy(pcol, pcol_s, pat_copy.at[1])]
    for c in to_smem:
        c.start()
    for c in to_smem:
        c.wait()

    def occupied(q, k):
        if q < 2:
            return prow_s[lax.div(k, 2), 0, q * 2 + lax.rem(k, 2)]
        return pcol_s[lax.div(k, 2), 0, lax.rem(k, 2) * 2 + (q - 2)]

    def backward(n, carry):
        k = NB - 1 - n
        later = []
        for q in range(4):
            nxt[q, k] = carry[q]
            later.append(carry[q] + occupied(q, k) * (k - carry[q]))
        return tuple(later)

    for q in range(4):
        nxt[q, NB] = NB
    first = lax.fori_loop(0, NB, backward, (jnp.int32(NB),) * 4)

    def forward(t, carry):
        later = []
        for q in range(4):
            idx[q, t] = carry[q]
            later.append(nxt[q, carry[q]])
        return tuple(later)

    lax.fori_loop(0, SLOTS, forward, first)

    def count(k, carry):
        later = []
        for j in range(2):
            is_on = occupied(2 + j, k)
            rank[j, k] = SLOTS + is_on * (carry[j] - SLOTS)
            later.append(carry[j] + is_on)
        return tuple(later)

    for j in range(2):
        rank[j, NB] = SLOTS
    lax.fori_loop(0, NB, count, (jnp.int32(0),) * 2)

    def unit(j, da, db):
        dx, dy = (da, db) if j == 0 else (db, da)
        return lax.rem(y + dy + 4, 4) * 4 + lax.rem(x + dx + 4, 4)

    order = {0: 0, -1: 1, 1: 2, 2: 3}

    def column_send(j, q, half, axis, s, n):
        slots = pl.ds(0, SLOTS) if half is None else pl.ds(half * (SLOTS // 2), SLOTS // 2)
        ref = cpanel[j].at[q, slots]
        send(ref, ref, c_send.at[j], c_recv.at[j, n], xy_side(axis, s))

    def column_wait(j, q, half, n):
        slots = pl.ds(0, SLOTS) if half is None else pl.ds(half * (SLOTS // 2), SLOTS // 2)
        wait_for(cpanel[j].at[q, slots], c_recv.at[j, n])

    def column_along(j, da):
        for way, s in enumerate((1, -1)):
            column_send(j, unit(j, da, 0), None, 1 - j, s, 4 + order[da] * 2 + way)

    def column_own(j):
        def body(t, _):
            cpanel[j][part_xy, t] = crecv[idx[2 + j, t], :, j * SIZE : (j + 1) * SIZE]
            return 0

        lax.fori_loop(0, SLOTS, body, 0)

    def column_start():
        wait_for(crecv.at[pl.ds(0, NB)], col_recv)
        for j in range(2):
            column_own(j)
            for way, s in enumerate((1, -1)):
                column_send(j, unit(j, 0, 0), None, j, s, way)
        for j in range(2):
            column_along(j, 0)

    def column_near(j, s):
        way = (1 - s) // 2
        column_wait(j, unit(j, -s, 0), None, way)
        column_send(j, unit(j, -s, 0), way, j, s, 2 + way)
        column_along(j, -s)

    def column_far(j):
        for way in range(2):
            column_wait(j, unit(j, 2, 0), way, 2 + way)
        column_along(j, 2)

    def column_second(j, da, s):
        column_wait(j, unit(j, da, -s), None, 4 + order[da] * 2 + (1 - s) // 2)
        if (da in (0, -1)) == (s == 1):
            column_send(j, unit(j, da, -s), None, 1 - j, s, 12 + order[da])

    def column_last(j):
        for da in order:
            column_wait(j, unit(j, da, 2), None, 12 + order[da])

    def slices(stage, c, d, part=None):
        here = panel.at[stage, c, lax.rem(z + d + 8, 8) * 2 + core]
        return here if part is None else here.at[:, pl.ds(part * (SLOTS // 2 * HALF), SLOTS // 2 * HALF)]

    def ring_send(stage, c, d, s, part=None):
        ref = slices(stage, c, -s * d, part)
        send(ref, ref, z_send.at[stage, c], z_recv.at[stage, c, (1 - s) // 2, d], z_side(s))

    def to_mate(stage, c, d):
        ref = slices(stage, c, d)
        send(ref, ref, z_send.at[stage, c], mate_recv.at[stage, c], {"row": pair + 1 - core, "col": col})

    def ring_start(stage, c):
        received = (rrecv, srecv)[stage][c]
        wait_for(received.at[pl.ds(0, NB)], (row_recv, s_recv)[stage].at[c])

        def body(t, _):
            panel[stage, c, part_z, :, pl.ds(pl.multiple_of(t * HALF, HALF), HALF)] = received[idx[c // 2, t]]
            return 0

        lax.fori_loop(0, SLOTS, body, 0)
        for s in (1, -1):
            ring_send(stage, c, 0, s)
        to_mate(stage, c, 0)

    def ring_hop(stage, c, d):
        for way, s in enumerate((1, -1)):
            wait_for(slices(stage, c, -s * d), z_recv.at[stage, c, way, d - 1])
            ring_send(stage, c, d, s, None if d < 3 else way)
        for s in (1, -1):
            to_mate(stage, c, -s * d)

    def ring_last(stage, c):
        for way in range(2):
            wait_for(slices(stage, c, 4, way), z_recv.at[stage, c, way, 3])
        to_mate(stage, c, 4)

    def ring_end(stage, c):
        wait_for(panel.at[stage, c, pl.ds(0, 8)], mate_recv.at[stage, c])

    def gather_rhs(i):
        def body(t, _):
            k = idx[i, t]
            for j in range(2):
                slot = rank[j, k]
                for h in range(2):
                    block = cpanel[j][h * 8 : h * 8 + 8, slot]
                    rhs[2 * i + h, pl.ds(pl.multiple_of(t * HALF, HALF), HALF), j * SIZE : (j + 1) * SIZE] = block.reshape(HALF, SIZE)
            return 0

        lax.fori_loop(0, SLOTS, body, 0)

    def product(stage, c):
        ring_end(stage, c)
        return jnp.dot(panel[stage, c].reshape(SIZE, SLOTS * HALF), rhs[c], preferred_element_type=F32)

    def keep(i, j):
        return prow_s[part_z, 0, i * 2 + j].astype(F32)

    def square(c):
        i = c // 2
        if c % 2 == 0:
            sf[i] = product(0, c)
            return
        value = sf[i] + product(0, c)
        for j in range(2):
            kept = value[:, j * SIZE : (j + 1) * SIZE] * keep(i, j)
            sf[i, :, j * SIZE : (j + 1) * SIZE] = kept
            sl[i, j] = kept.astype(BF16)
        for h in range(2):
            def body(n, _):
                d = lax.rem(n + 7, GROUP)
                s, device = mate_target(d)
                deliver(d, sl.at[i, :, pl.ds(pl.multiple_of(s * PART, PART), PART), half(h)], srecv[2 * i + h].at[pl.ds(2 * part_z, 2)], s_send.at[i], s_recv.at[2 * i + h], device, True)
                return 0

            lax.fori_loop(0, GROUP, body, 0)

    def cube(c):
        i = c // 2
        if c % 2 == 0:
            cf[i] = product(1, c)
            return
        whole = cf[i] + product(1, c)
        value = jnp.concatenate([whole[:, j * SIZE : (j + 1) * SIZE] * keep(i, j) for j in range(2)], axis=1)
        value = (3.0 * sf[i] - 2.0 * value).astype(BF16)

        @pl.when(settled)
        def _():
            out[i] = value

        @pl.when(jnp.logical_not(settled))
        def _():
            obuf[i] = value
            send(obuf.at[i], out.at[i], out_sem.at[0, i], out_sem.at[1, i], {"row": pair + xl, "col": part_z})

    ring_start(0, 0)
    column_start()
    ring_start(0, 1)
    ring_start(0, 2)
    column_near(0, 1)
    column_near(0, -1)
    ring_hop(0, 0, 1)
    column_near(1, 1)
    column_near(1, -1)
    ring_hop(0, 1, 1)
    ring_start(0, 3)
    ring_hop(0, 2, 1)
    column_second(1, 0, 1)
    ring_hop(0, 0, 2)
    column_second(1, 0, -1)
    column_second(0, 0, 1)
    column_second(0, 0, -1)
    ring_hop(0, 1, 2)
    column_far(0)
    column_second(0, -1, 1)
    ring_hop(0, 3, 1)
    column_second(0, -1, -1)
    column_second(1, -1, 1)
    column_second(1, -1, -1)
    column_second(0, 1, 1)
    ring_hop(0, 2, 2)
    column_second(0, 1, -1)
    column_second(1, 1, 1)
    column_second(1, 1, -1)
    ring_hop(0, 0, 3)
    column_far(1)
    ring_hop(0, 1, 3)
    column_second(0, 2, -1)
    ring_hop(0, 3, 2)
    ring_hop(0, 2, 3)
    ring_last(0, 0)
    column_second(0, 2, 1)
    ring_last(0, 1)
    ring_hop(0, 3, 3)
    ring_last(0, 2)
    column_second(1, 2, 1)
    column_second(1, 2, -1)
    column_last(0)
    ring_last(0, 3)
    column_last(1)
    gather_rhs(0)
    square(0)
    square(1)
    gather_rhs(1)
    square(2)
    square(3)
    ring_start(1, 0)
    ring_start(1, 1)
    ring_start(1, 2)
    ring_hop(1, 0, 1)
    ring_hop(1, 1, 1)
    ring_start(1, 3)
    ring_hop(1, 2, 1)
    ring_hop(1, 0, 2)
    ring_hop(1, 1, 2)
    ring_hop(1, 3, 1)
    ring_hop(1, 2, 2)
    ring_hop(1, 0, 3)
    ring_hop(1, 1, 3)
    ring_hop(1, 3, 2)
    ring_hop(1, 2, 3)
    ring_last(1, 0)
    ring_last(1, 1)
    ring_hop(1, 3, 3)
    ring_last(1, 2)
    cube(0)
    cube(1)
    ring_last(1, 3)
    cube(2)
    cube(3)

    @pl.when(jnp.logical_not(settled))
    def _():
        for i in range(2):
            wait_for(out.at[i], out_sem.at[1, i])
            wait_for(obuf.at[i], out_sem.at[0, i])
        for c in range(4):
            wait_for(rrecv[c].at[pl.ds(0, 2)], a2a_send.at[0])
        wait_for(crecv.at[pl.ds(0, 2)], a2a_send.at[1])
        wait_for(prow.at[0], a2a_send.at[2])
        wait_for(pcol.at[0], a2a_send.at[2])

    for c in range(4):
        wait_for(rrecv[c].at[pl.ds(0, 30)], a2a_send.at[0])
    wait_for(crecv.at[pl.ds(0, 30)], a2a_send.at[1])
    wait_for(prow.at[pl.ds(1, 15)], a2a_send.at[2])
    wait_for(pcol.at[pl.ds(1, 15)], a2a_send.at[2])
    for c in range(4):
        wait_for(srecv[c].at[pl.ds(0, 30)], s_send.at[c // 2])
        for stage in range(2):
            wait_for(panel.at[stage, c, pl.ds(0, 15)], z_send.at[stage, c])
    for j in range(2):
        wait_for(cpanel[j].at[pl.ds(0, 15), pl.ds(0, SLOTS)], c_send.at[j])


def shards(density, pattern):
    vmem, smem, dma = pltpu.VMEM, pltpu.SMEM, pltpu.SemaphoreType.DMA
    received = [vmem((NB + 1, PART, HALF), BF16)] * 4
    panel = vmem((GROUP, SLOTS + 1, PART, SIZE), BF16)
    purified = pl.pallas_call(
        kernel,
        out_shape=jax.ShapeDtypeStruct((2, SIZE, 2 * SIZE), BF16),
        in_specs=[pl.BlockSpec(memory_space=pl.ANY)] * 2,
        out_specs=pl.BlockSpec(memory_space=vmem),
        scratch_shapes=[
            vmem((2, 2, SIZE, SIZE), BF16),
            smem((2, 2), jnp.int32),
            *received, *received,
            vmem((NB + 1, PART, 2 * SIZE), BF16),
            vmem((2, 4, GROUP, PART, SLOTS * HALF), BF16),
            panel, panel,
            vmem((4, SLOTS * HALF, 2 * SIZE), BF16),
            vmem((2, SIZE, 2 * SIZE), F32),
            vmem((2, SIZE, 2 * SIZE), F32),
            vmem((2, 2, SIZE, SIZE), BF16),
            vmem((2, SIZE, 2 * SIZE), BF16),
            vmem((1, 128), jnp.int32),
            vmem((GROUP, 1, 128), jnp.int32),
            vmem((GROUP, 1, 128), jnp.int32),
            smem((GROUP, 1, 128), jnp.int32),
            smem((GROUP, 1, 128), jnp.int32),
            smem((4, NB + 1), jnp.int32),
            smem((4, SLOTS), jnp.int32),
            smem((2, NB + 1), jnp.int32),
            dma((5,)), dma((3,)), dma((4,)), dma, dma((2,)), dma((2,)),
            dma((2,)), dma((4,)), dma((2, 4)), dma((2, 4, 2, 4)), dma((2, 4)),
            dma((2,)), dma((2, 16)), dma((2, 2)),
        ],
        compiler_params=pltpu.CompilerParams(collective_id=0, has_side_effects=True, vmem_limit_bytes=48 * 2**20),
        name="purify",
    )(density.reshape(2, SIZE, 2 * SIZE), pattern)
    return purified.reshape(2 * SIZE, 2 * SIZE)


def solution(mesh):
    return jax.shard_map(
        shards,
        mesh=mesh,
        in_specs=(P("row", "col"), P("row", "col")),
        out_specs=P("row", "col"),
        check_vma=False,
    )
```

time: 94.9 us -> 88.9 us (0.937)
  Pallas kernels: 92.3 us -> 86.3 us
    pallas_call x1, Pallas kernels: 92.3 us -> 86.3 us  [shards(): pl.pallas_call(kernel, out_shape=jax.ShapeDtypeStruct((2, SIZE, 2 * SIZE)...]
where the time goes in v2:
time: 88.9 us; the launch traced here: 88.8 us
  Pallas kernels  86.3 us (97%)
  local copies, waits for them, and re-layouts  2.52 us (3%)
    pallas_call x1, Pallas kernels, shards(): pl.pallas_call(kernel, out_shape=jax.ShapeDtypeStruct((2, SIZE, 2 * SIZE)...  86.3 us
    unnamed x5, local copies, waits for them, and re-layouts  2.52 us

profile of v2, /device:TPU:1, one launch (start us, length us, event | category | flops | bytes accessed | tf_op | source)
XLA Modules:
  0.0 88.8 jit_solution(16975796370596249020)
XLA Ops:
  0.0 0.0 copy-start.1
  0.0 0.7 copy-done.1
  0.7 0.0 copy-start
  0.7 1.0 %copy-done = bf16[512,512]{1,0:T(8,128)(2,1)S(1)} copy-done((bf16[512,512]{1,0:T(8,128)(2,1)S(1)}, bf16[512,512]{1,0:T(8,128)(2,1)}, u32[]{:S(2)}) %copy-start) | copy-done | bytes 524312
  1.7 86.3 %purify.1 = bf16[2,256,512]{2,1,0:T(8,128)(2,1)S(1)} custom-call(bf16[2,256,512]{2,1,0:T(8,128)(2,1)S(1)} %bitcast.3, s32[2,2]{1,0:T(2,128)S(1)} %copy-done.1), custom_call_target="tpu_custom_call" | custom-call | tf_op jit(solution)/shard_map/purify/pallas_call | solution.py:450
  88.0 0.8 copy.4
Async XLA Ops:
  0.0 0.7 copy-start.1
  0.7 1.0 %copy-start = (bf16[512,512]{1,0:T(8,128)(2,1)S(1)}, bf16[512,512]{1,0:T(8,128)(2,1)}, u32[]{:S(2)}) copy-start(bf16[512,512]{1,0:T(8,128)(2,1)} %param.2) | copy-start | bytes 1572868

commit v3 on v2

--- a/solution.py
+++ b/solution.py
@@ -22,8 +22,8 @@
     return {"row": (y * 2 + lax.div(x, 2)) * 2 + core, "col": z * 2 + lax.rem(x, 2)}
 
 
-def kernel(dens, patt_hbm, out, blocks, patt, rr0, rr1, rr2, rr3, sr0, sr1, sr2, sr3, crecv, panel, cp0, cp1, rhs, sf, cf, sl, obuf, pmsg, prow, pcol, prow_s, pcol_s, nxt, idx, rank, load_sem, a2a_send, row_recv, col_recv, pat_recv, pat_copy, s_send, s_recv, z_send, z_recv, mate_recv, c_send, c_recv, out_sem):
-    rrecv, srecv, cpanel = (rr0, rr1, rr2, rr3), (sr0, sr1, sr2, sr3), (cp0, cp1)
+def kernel(dens, patt_hbm, out, blocks, patt, rr0, rr1, rr2, rr3, sr0, sr1, sr2, sr3, crecv, panel, square_panel, cp0, cp1, cp2, cp3, rhs, sf, smate, cf, sl, obuf, pmsg, prow, pcol, pmate, prow_s, pcol_s, pmate_s, nxt, idx, rank, load_sem, a2a_send, row_recv, col_recv, pat_recv, pat_copy, s_send, s_recv, z_send, z_recv, mate_recv, share_send, share_recv, c_send, c_recv, out_send, out_recv):
+    rrecv, srecv, cpanel = (rr0, rr1, rr2, rr3), (sr0, sr1, sr2, sr3), (cp0, cp1, cp2, cp3)
     row, col = lax.axis_index("row"), lax.axis_index("col")
     y, xh, core = lax.div(row, 4), lax.rem(lax.div(row, 2), 2), lax.rem(row, 2)
     z, xl = lax.div(col, 2), lax.rem(col, 2)
@@ -45,6 +45,8 @@
         zz, cc = lax.rem(z + lax.div(d, 2), 8), lax.rem(core + d, 2)
         return zz * 2 + cc, {"row": pair + cc, "col": zz * 2 + xl}
 
+    mate = {"row": pair + 1 - core, "col": col}
+
     def z_side(s):
         return place(x, y, lax.rem(z + s + 8, 8), core)
 
@@ -143,11 +145,12 @@
     for received in (*rrecv, *srecv):
         received[NB] = jnp.zeros((PART, HALF), BF16)
     crecv[NB] = jnp.zeros((PART, 2 * SIZE), BF16)
-    for j in range(2):
+    for j in range(4):
         cpanel[j][:, SLOTS] = jnp.zeros((GROUP, PART, SIZE), BF16)
 
     wait_for(prow, pat_recv.at[0])
     wait_for(pcol, pat_recv.at[1])
+    send(pcol, pmate, share_send.at[4], share_recv.at[4], mate)
     to_smem = [pltpu.make_async_copy(prow, prow_s, pat_copy.at[0]), pltpu.make_async_copy(pcol, pcol_s, pat_copy.at[1])]
     for c in to_smem:
         c.start()
@@ -180,17 +183,20 @@
 
     lax.fori_loop(0, SLOTS, forward, first)
 
-    def count(k, carry):
-        later = []
-        for j in range(2):
-            is_on = occupied(2 + j, k)
-            rank[j, k] = SLOTS + is_on * (carry[j] - SLOTS)
-            later.append(carry[j] + is_on)
-        return tuple(later)
-
-    for j in range(2):
-        rank[j, NB] = SLOTS
-    lax.fori_loop(0, NB, count, (jnp.int32(0),) * 2)
+    def ranks(group, table):
+        def count(k, carry):
+            later = []
+            for j in range(2):
+                is_on = table[lax.div(k, 2), 0, lax.rem(k, 2) * 2 + j]
+                rank[2 * group + j, k] = SLOTS + is_on * (carry[j] - SLOTS)
+                later.append(carry[j] + is_on)
+            return tuple(later)
+
+        for j in range(2):
+            rank[2 * group + j, NB] = SLOTS
+        lax.fori_loop(0, NB, count, (jnp.int32(0),) * 2)
+
+    ranks(0, pcol_s)
 
     def unit(j, da, db):
         dx, dy = (da, db) if j == 0 else (db, da)
@@ -246,9 +252,21 @@
     def column_last(j):
         for da in order:
             column_wait(j, unit(j, da, 2), None, 12 + order[da])
+        ref = pl.ds(0, SLOTS)
+        send(cpanel[j].at[:, ref], cpanel[2 + j].at[:, ref], share_send.at[j], share_recv.at[j], mate)
+
+    def shared_panels():
+        wait_for(pmate, share_recv.at[4])
+        copy = pltpu.make_async_copy(pmate, pmate_s, pat_copy.at[0])
+        copy.start()
+        copy.wait()
+        ranks(1, pmate_s)
+        for j in range(2):
+            wait_for(cpanel[2 + j].at[:, pl.ds(0, SLOTS)], share_recv.at[j])
 
     def slices(stage, c, d, part=None):
-        here = panel.at[stage, c, lax.rem(z + d + 8, 8) * 2 + core]
+        zz = lax.rem(z + d + 8, 8)
+        here = panel.at[c, zz * 2 + core] if stage == 0 else square_panel.at[c, zz]
         return here if part is None else here.at[:, pl.ds(part * (SLOTS // 2 * HALF), SLOTS // 2 * HALF)]
 
     def ring_send(stage, c, d, s, part=None):
@@ -256,15 +274,20 @@
         send(ref, ref, z_send.at[stage, c], z_recv.at[stage, c, (1 - s) // 2, d], z_side(s))
 
     def to_mate(stage, c, d):
-        ref = slices(stage, c, d)
-        send(ref, ref, z_send.at[stage, c], mate_recv.at[stage, c], {"row": pair + 1 - core, "col": col})
+        if stage == 0:
+            ref = slices(stage, c, d)
+            send(ref, ref, z_send.at[stage, c], mate_recv.at[c], mate)
 
     def ring_start(stage, c):
         received = (rrecv, srecv)[stage][c]
         wait_for(received.at[pl.ds(0, NB)], (row_recv, s_recv)[stage].at[c])
 
         def body(t, _):
-            panel[stage, c, part_z, :, pl.ds(pl.multiple_of(t * HALF, HALF), HALF)] = received[idx[c // 2, t]]
+            lanes = pl.ds(pl.multiple_of(t * HALF, HALF), HALF)
+            if stage == 0:
+                panel[c, part_z, :, lanes] = received[idx[c // 2, t]]
+            else:
+                square_panel[c, z, :, lanes] = received[idx[c // 2, t]]
             return 0
 
         lax.fori_loop(0, SLOTS, body, 0)
@@ -284,13 +307,10 @@
             wait_for(slices(stage, c, 4, way), z_recv.at[stage, c, way, 3])
         to_mate(stage, c, 4)
 
-    def ring_end(stage, c):
-        wait_for(panel.at[stage, c, pl.ds(0, 8)], mate_recv.at[stage, c])
-
-    def gather_rhs(i):
+    def gather_rhs(i, group):
         def body(t, _):
             k = idx[i, t]
-            for j in range(2):
+            for j in (2 * group, 2 * group + 1):
                 slot = rank[j, k]
                 for h in range(2):
                     block = cpanel[j][h * 8 : h * 8 + 8, slot]
@@ -299,22 +319,21 @@
 
         lax.fori_loop(0, SLOTS, body, 0)
 
-    def product(stage, c):
-        ring_end(stage, c)
-        return jnp.dot(panel[stage, c].reshape(SIZE, SLOTS * HALF), rhs[c], preferred_element_type=F32)
-
     def keep(i, j):
-        return prow_s[part_z, 0, i * 2 + j].astype(F32)
+        group = core if j < 2 else 1 - core
+        return prow_s[z * 2 + group, 0, i * 2 + j % 2].astype(F32)
 
     def square(c):
         i = c // 2
+        wait_for(panel.at[c, pl.ds(0, 8)], mate_recv.at[c])
+        value = jnp.dot(panel[c].reshape(SIZE, SLOTS * HALF), rhs[c, :, : 2 * SIZE], preferred_element_type=F32)
         if c % 2 == 0:
-            sf[i] = product(0, c)
+            sf[i] = value.reshape(8, 2, PART, 2 * SIZE)
             return
-        value = sf[i] + product(0, c)
+        value = sf[i].reshape(SIZE, 2 * SIZE) + value
         for j in range(2):
             kept = value[:, j * SIZE : (j + 1) * SIZE] * keep(i, j)
-            sf[i, :, j * SIZE : (j + 1) * SIZE] = kept
+            sf[i, :, :, :, j * SIZE : (j + 1) * SIZE] = kept.reshape(8, 2, PART, SIZE)
             sl[i, j] = kept.astype(BF16)
         for h in range(2):
             def body(n, _):
@@ -324,24 +343,31 @@
                 return 0
 
             lax.fori_loop(0, GROUP, body, 0)
+        send(sf.at[i, :, 1 - core], smate.at[i], share_send.at[2 + i], share_recv.at[2 + i], mate)
 
     def cube(c):
         i = c // 2
+        value = jnp.dot(square_panel[c].reshape(HALF, SLOTS * HALF), rhs[c], preferred_element_type=F32)
         if c % 2 == 0:
-            cf[i] = product(1, c)
+            cf[i] = value
             return
-        whole = cf[i] + product(1, c)
-        value = jnp.concatenate([whole[:, j * SIZE : (j + 1) * SIZE] * keep(i, j) for j in range(2)], axis=1)
-        value = (3.0 * sf[i] - 2.0 * value).astype(BF16)
+        wait_for(smate.at[i], share_recv.at[2 + i])
+        value = cf[i] + value
+        value = jnp.concatenate([value[:, j * SIZE : (j + 1) * SIZE] * keep(i, j) for j in range(4)], axis=1).reshape(8, PART, 4 * SIZE)
+        own = (3.0 * sf[i, :, core] - 2.0 * value[:, :, : 2 * SIZE]).astype(BF16)
+        other = (3.0 * smate[i] - 2.0 * value[:, :, 2 * SIZE :]).astype(BF16)
+        obuf[i, 1] = other
 
         @pl.when(settled)
         def _():
-            out[i] = value
+            send(obuf.at[i, 1], out.at[i, :, core], out_send, out_recv.at[i, core], {"row": row, "col": z * 2 + 1 - xl})
+            out[i, :, core] = own
 
         @pl.when(jnp.logical_not(settled))
         def _():
-            obuf[i] = value
-            send(obuf.at[i], out.at[i], out_sem.at[0, i], out_sem.at[1, i], {"row": pair + xl, "col": part_z})
+            obuf[i, 0] = own
+            send(obuf.at[i, 0], out.at[i, :, core], out_send, out_recv.at[i, core], {"row": pair + xl, "col": part_z})
+            send(obuf.at[i, 1], out.at[i, :, core], out_send, out_recv.at[i, core], mate)
 
     ring_start(0, 0)
     column_start()
@@ -388,42 +414,48 @@
     column_last(0)
     ring_last(0, 3)
     column_last(1)
-    gather_rhs(0)
+    gather_rhs(0, 0)
     square(0)
     square(1)
-    gather_rhs(1)
+    gather_rhs(1, 0)
     square(2)
     square(3)
     ring_start(1, 0)
     ring_start(1, 1)
+    shared_panels()
+    gather_rhs(0, 1)
     ring_start(1, 2)
+    gather_rhs(1, 1)
+    ring_start(1, 3)
     ring_hop(1, 0, 1)
     ring_hop(1, 1, 1)
-    ring_start(1, 3)
     ring_hop(1, 2, 1)
+    ring_hop(1, 3, 1)
     ring_hop(1, 0, 2)
     ring_hop(1, 1, 2)
-    ring_hop(1, 3, 1)
     ring_hop(1, 2, 2)
+    ring_hop(1, 3, 2)
     ring_hop(1, 0, 3)
     ring_hop(1, 1, 3)
-    ring_hop(1, 3, 2)
     ring_hop(1, 2, 3)
+    ring_hop(1, 3, 3)
     ring_last(1, 0)
     ring_last(1, 1)
-    ring_hop(1, 3, 3)
-    ring_last(1, 2)
     cube(0)
     cube(1)
+    ring_last(1, 2)
     ring_last(1, 3)
     cube(2)
     cube(3)
 
+    for i in range(2):
+        wait_for(out.at[i, :, 1 - core], out_recv.at[i, 1 - core])
+
     @pl.when(jnp.logical_not(settled))
     def _():
         for i in range(2):
-            wait_for(out.at[i], out_sem.at[1, i])
-            wait_for(obuf.at[i], out_sem.at[0, i])
+            wait_for(out.at[i, :, core], out_recv.at[i, core])
+            wait_for(obuf.at[i, 0], out_send)
         for c in range(4):
             wait_for(rrecv[c].at[pl.ds(0, 2)], a2a_send.at[0])
         wait_for(crecv.at[pl.ds(0, 2)], a2a_send.at[1])
@@ -435,11 +467,16 @@
     wait_for(crecv.at[pl.ds(0, 30)], a2a_send.at[1])
     wait_for(prow.at[pl.ds(1, 15)], a2a_send.at[2])
     wait_for(pcol.at[pl.ds(1, 15)], a2a_send.at[2])
+    for i in range(2):
+        wait_for(obuf.at[i, 1], out_send)
+        wait_for(smate.at[i], share_send.at[2 + i])
     for c in range(4):
         wait_for(srecv[c].at[pl.ds(0, 30)], s_send.at[c // 2])
-        for stage in range(2):
-            wait_for(panel.at[stage, c, pl.ds(0, 15)], z_send.at[stage, c])
+        wait_for(panel.at[c, pl.ds(0, 15)], z_send.at[0, c])
+        wait_for(square_panel.at[c, pl.ds(0, 7)], z_send.at[1, c])
+    wait_for(pcol, share_send.at[4])
     for j in range(2):
+        wait_for(cpanel[j].at[:, pl.ds(0, SLOTS)], share_send.at[j])
         wait_for(cpanel[j].at[pl.ds(0, 15), pl.ds(0, SLOTS)], c_send.at[j])
 
 
@@ -449,7 +486,7 @@
     panel = vmem((GROUP, SLOTS + 1, PART, SIZE), BF16)
     purified = pl.pallas_call(
         kernel,
-        out_shape=jax.ShapeDtypeStruct((2, SIZE, 2 * SIZE), BF16),
+        out_shape=jax.ShapeDtypeStruct((2, 8, 2, PART, 2 * SIZE), BF16),
         in_specs=[pl.BlockSpec(memory_space=pl.ANY)] * 2,
         out_specs=pl.BlockSpec(memory_space=vmem),
         scratch_shapes=[
@@ -457,24 +494,28 @@
             smem((2, 2), jnp.int32),
             *received, *received,
             vmem((NB + 1, PART, 2 * SIZE), BF16),
-            vmem((2, 4, GROUP, PART, SLOTS * HALF), BF16),
-            panel, panel,
-            vmem((4, SLOTS * HALF, 2 * SIZE), BF16),
-            vmem((2, SIZE, 2 * SIZE), F32),
-            vmem((2, SIZE, 2 * SIZE), F32),
+            vmem((4, GROUP, PART, SLOTS * HALF), BF16),
+            vmem((4, 8, PART, SLOTS * HALF), BF16),
+            panel, panel, panel, panel,
+            vmem((4, SLOTS * HALF, 4 * SIZE), BF16),
+            vmem((2, 8, 2, PART, 2 * SIZE), F32),
+            vmem((2, 8, PART, 2 * SIZE), F32),
+            vmem((2, HALF, 4 * SIZE), F32),
             vmem((2, 2, SIZE, SIZE), BF16),
-            vmem((2, SIZE, 2 * SIZE), BF16),
+            vmem((2, 2, 8, PART, 2 * SIZE), BF16),
             vmem((1, 128), jnp.int32),
+            vmem((GROUP, 1, 128), jnp.int32),
             vmem((GROUP, 1, 128), jnp.int32),
             vmem((GROUP, 1, 128), jnp.int32),
             smem((GROUP, 1, 128), jnp.int32),
             smem((GROUP, 1, 128), jnp.int32),
+            smem((GROUP, 1, 128), jnp.int32),
             smem((4, NB + 1), jnp.int32),
             smem((4, SLOTS), jnp.int32),
-            smem((2, NB + 1), jnp.int32),
+            smem((4, NB + 1), jnp.int32),
             dma((5,)), dma((3,)), dma((4,)), dma, dma((2,)), dma((2,)),
-            dma((2,)), dma((4,)), dma((2, 4)), dma((2, 4, 2, 4)), dma((2, 4)),
-            dma((2,)), dma((2, 16)), dma((2, 2)),
+            dma((2,)), dma((4,)), dma((2, 4)), dma((2, 4, 2, 4)), dma((4,)), dma((5,)), dma((5,)),
+            dma((2,)), dma((2, 16)), dma, dma((2, 2)),
         ],
         compiler_params=pltpu.CompilerParams(collective_id=0, has_side_effects=True, vmem_limit_bytes=48 * 2**20),
         name="purify",

time: 88.9 us -> 85.8 us (0.965)
  Pallas kernels: 86.3 us -> 83.1 us
    pallas_call x1, Pallas kernels: 86.3 us -> 83.1 us  [shards(): pl.pallas_call(kernel, out_shape=jax.ShapeDtypeStruct((2, 8, 2, PART, 2 *...]
where the time goes in v3:
time: 85.8 us; the launch traced here: 85.7 us
  Pallas kernels  83.1 us (97%)
  local copies, waits for them, and re-layouts  2.52 us (3%)
    pallas_call x1, Pallas kernels, shards(): pl.pallas_call(kernel, out_shape=jax.ShapeDtypeStruct((2, 8, 2, PART, 2 *...  83.1 us
    unnamed x5, local copies, waits for them, and re-layouts  2.52 us

profile of v3, /device:TPU:1, one launch (start us, length us, event | category | flops | bytes accessed | tf_op | source)
XLA Modules:
  0.0 85.7 jit_solution(16874621058685276927)
XLA Ops:
  0.0 0.0 copy-start.1
  0.0 0.7 copy-done.1
  0.7 0.0 copy-start
  0.7 1.0 %copy-done = bf16[512,512]{1,0:T(8,128)(2,1)S(1)} copy-done((bf16[512,512]{1,0:T(8,128)(2,1)S(1)}, bf16[512,512]{1,0:T(8,128)(2,1)}, u32[]{:S(2)}) %copy-start) | copy-done | bytes 524312
  1.7 83.1 %purify.1 = bf16[2,8,2,16,512]{4,3,2,1,0:T(8,128)(2,1)S(1)} custom-call(bf16[2,256,512]{2,1,0:T(8,128)(2,1)S(1)} %bitcast.3, s32[2,2]{1,0:T(2,128)S(1)} %copy-done.1), custom_call_target="tpu_custom_call" | custom-call | tf_op jit(solution)/shard_map/purify/pallas_call | solution.py:487
  84.9 0.8 copy.4
Async XLA Ops:
  0.0 0.7 copy-start.1
  0.7 1.0 %copy-start = (bf16[512,512]{1,0:T(8,128)(2,1)S(1)}, bf16[512,512]{1,0:T(8,128)(2,1)}, u32[]{:S(2)}) copy-start(bf16[512,512]{1,0:T(8,128)(2,1)} %param.2) | copy-start | bytes 1572868

commit v4 on v3

--- a/solution.py
+++ b/solution.py
@@ -22,7 +22,7 @@
     return {"row": (y * 2 + lax.div(x, 2)) * 2 + core, "col": z * 2 + lax.rem(x, 2)}
 
 
-def kernel(dens, patt_hbm, out, blocks, patt, rr0, rr1, rr2, rr3, sr0, sr1, sr2, sr3, crecv, panel, square_panel, cp0, cp1, cp2, cp3, rhs, sf, smate, cf, sl, obuf, pmsg, prow, pcol, pmate, prow_s, pcol_s, pmate_s, nxt, idx, rank, load_sem, a2a_send, row_recv, col_recv, pat_recv, pat_copy, s_send, s_recv, z_send, z_recv, mate_recv, share_send, share_recv, c_send, c_recv, out_send, out_recv):
+def kernel(dens, patt_hbm, out, blocks, patt, rr0, rr1, rr2, rr3, sr0, sr1, sr2, sr3, crecv, panel, square_panel, cp0, cp1, cp2, cp3, rhs, sf, final, sl, obuf, pmsg, prow, pcol, pmate, prow_s, pcol_s, pmate_s, nxt, idx, rank, load_sem, a2a_send, row_recv, col_recv, pat_recv, pat_copy, s_send, s_recv, z_send, z_recv, mate_recv, share_send, share_recv, c_send, c_recv, out_send, out_recv):
     rrecv, srecv, cpanel = (rr0, rr1, rr2, rr3), (sr0, sr1, sr2, sr3), (cp0, cp1, cp2, cp3)
     row, col = lax.axis_index("row"), lax.axis_index("col")
     y, xh, core = lax.div(row, 4), lax.rem(lax.div(row, 2), 2), lax.rem(row, 2)
@@ -273,9 +273,9 @@
         ref = slices(stage, c, -s * d, part)
         send(ref, ref, z_send.at[stage, c], z_recv.at[stage, c, (1 - s) // 2, d], z_side(s))
 
-    def to_mate(stage, c, d):
+    def to_mate(stage, c, d, part=None):
         if stage == 0:
-            ref = slices(stage, c, d)
+            ref = slices(stage, c, d, part)
             send(ref, ref, z_send.at[stage, c], mate_recv.at[c], mate)
 
     def ring_start(stage, c):
@@ -305,7 +305,7 @@
     def ring_last(stage, c):
         for way in range(2):
             wait_for(slices(stage, c, 4, way), z_recv.at[stage, c, way, 3])
-        to_mate(stage, c, 4)
+            to_mate(stage, c, 4, way)
 
     def gather_rhs(i, group):
         def body(t, _):
@@ -343,31 +343,45 @@
                 return 0
 
             lax.fori_loop(0, GROUP, body, 0)
-        send(sf.at[i, :, 1 - core], smate.at[i], share_send.at[2 + i], share_recv.at[2 + i], mate)
-
-    def cube(c):
-        i = c // 2
-        value = jnp.dot(square_panel[c].reshape(HALF, SLOTS * HALF), rhs[c], preferred_element_type=F32)
-        if c % 2 == 0:
-            cf[i] = value
-            return
-        wait_for(smate.at[i], share_recv.at[2 + i])
-        value = cf[i] + value
-        value = jnp.concatenate([value[:, j * SIZE : (j + 1) * SIZE] * keep(i, j) for j in range(4)], axis=1).reshape(8, PART, 4 * SIZE)
-        own = (3.0 * sf[i, :, core] - 2.0 * value[:, :, : 2 * SIZE]).astype(BF16)
-        other = (3.0 * smate[i] - 2.0 * value[:, :, 2 * SIZE :]).astype(BF16)
-        obuf[i, 1] = other
-
-        @pl.when(settled)
-        def _():
-            send(obuf.at[i, 1], out.at[i, :, core], out_send, out_recv.at[i, core], {"row": row, "col": z * 2 + 1 - xl})
-            out[i, :, core] = own
-
-        @pl.when(jnp.logical_not(settled))
-        def _():
-            obuf[i, 0] = own
-            send(obuf.at[i, 0], out.at[i, :, core], out_send, out_recv.at[i, core], {"row": pair + xl, "col": part_z})
-            send(obuf.at[i, 1], out.at[i, :, core], out_send, out_recv.at[i, core], mate)
+        send(sf.at[i, :, 1 - core], final.at[i, 1], share_send.at[2 + i], share_recv.at[2 + i], mate)
+
+    def cube_rows(i, reach):
+        here = [lax.rem(z + d + 8, 8) for d in reach]
+        lhs = [jnp.concatenate([square_panel[c, zz] for zz in here], axis=0) for c in (2 * i, 2 * i + 1)]
+        for step in range(2):
+            group = jnp.where(settled, 1 - step, step)
+            lanes = pl.ds(pl.multiple_of(group * 2 * SIZE, 2 * SIZE), 2 * SIZE)
+            value = sum(jnp.dot(lhs[h], rhs[2 * i + h, :, lanes], preferred_element_type=F32) for h in range(2))
+            holder = z * 2 + jnp.where(group == 0, core, 1 - core)
+            kept = [value[:, j * SIZE : (j + 1) * SIZE] * prow_s[holder, 0, i * 2 + j].astype(F32) for j in range(2)]
+            value = jnp.concatenate(kept, axis=1)
+            done = []
+            for n, zz in enumerate(here):
+                done.append((3.0 * final[i, group, zz] - 2.0 * value[n * PART : (n + 1) * PART]).astype(BF16))
+            if step == 0:
+                for zz, rows in zip(here, done):
+                    obuf[i, 0, zz] = rows
+                    send(obuf.at[i, 0, zz], out.at[i, zz, core], out_send, out_recv.at[i, core], {"row": pair + xl, "col": z * 2 + 1 - xl})
+                continue
+
+            @pl.when(settled)
+            def _():
+                for zz, rows in zip(here, done):
+                    out[i, zz, core] = rows
+
+            @pl.when(jnp.logical_not(settled))
+            def _():
+                for zz, rows in zip(here, done):
+                    obuf[i, 1, zz] = rows
+                    send(obuf.at[i, 1, zz], out.at[i, zz, core], out_send, out_recv.at[i, core], mate)
+
+    def cube_early(i):
+        wait_for(final.at[i, 1], share_recv.at[2 + i])
+        final[i, 0] = sf[i, :, core]
+        cube_rows(i, (0, 1, -1, 2, -2))
+
+    def cube_late(i):
+        cube_rows(i, (3, -3, 4))
 
     ring_start(0, 0)
     column_start()
@@ -435,18 +449,18 @@
     ring_hop(1, 1, 2)
     ring_hop(1, 2, 2)
     ring_hop(1, 3, 2)
+    cube_early(0)
     ring_hop(1, 0, 3)
     ring_hop(1, 1, 3)
     ring_hop(1, 2, 3)
     ring_hop(1, 3, 3)
+    cube_early(1)
     ring_last(1, 0)
     ring_last(1, 1)
-    cube(0)
-    cube(1)
+    cube_late(0)
     ring_last(1, 2)
     ring_last(1, 3)
-    cube(2)
-    cube(3)
+    cube_late(1)
 
     for i in range(2):
         wait_for(out.at[i, :, 1 - core], out_recv.at[i, 1 - core])
@@ -455,7 +469,7 @@
     def _():
         for i in range(2):
             wait_for(out.at[i, :, core], out_recv.at[i, core])
-            wait_for(obuf.at[i, 0], out_send)
+            wait_for(obuf.at[i, 1], out_send)
         for c in range(4):
             wait_for(rrecv[c].at[pl.ds(0, 2)], a2a_send.at[0])
         wait_for(crecv.at[pl.ds(0, 2)], a2a_send.at[1])
@@ -468,8 +482,8 @@
     wait_for(prow.at[pl.ds(1, 15)], a2a_send.at[2])
     wait_for(pcol.at[pl.ds(1, 15)], a2a_send.at[2])
     for i in range(2):
-        wait_for(obuf.at[i, 1], out_send)
-        wait_for(smate.at[i], share_send.at[2 + i])
+        wait_for(obuf.at[i, 0], out_send)
+        wait_for(final.at[i, 1], share_send.at[2 + i])
     for c in range(4):
         wait_for(srecv[c].at[pl.ds(0, 30)], s_send.at[c // 2])
         wait_for(panel.at[c, pl.ds(0, 15)], z_send.at[0, c])
@@ -499,8 +513,7 @@
             panel, panel, panel, panel,
             vmem((4, SLOTS * HALF, 4 * SIZE), BF16),
             vmem((2, 8, 2, PART, 2 * SIZE), F32),
-            vmem((2, 8, PART, 2 * SIZE), F32),
-            vmem((2, HALF, 4 * SIZE), F32),
+            vmem((2, 2, 8, PART, 2 * SIZE), F32),
             vmem((2, 2, SIZE, SIZE), BF16),
             vmem((2, 2, 8, PART, 2 * SIZE), BF16),
             vmem((1, 128), jnp.int32),

time: 85.8 us -> 84.5 us (0.985)
  Pallas kernels: 83.1 us -> 81.8 us
    pallas_call x1, Pallas kernels: 83.1 us -> 81.8 us  [shards(): pl.pallas_call(kernel, out_shape=jax.ShapeDtypeStruct((2, 8, 2, PART, 2 *...]
where the time goes in v4:
time: 84.5 us; the launch traced here: 84.3 us
  Pallas kernels  81.8 us (97%)
  local copies, waits for them, and re-layouts  2.52 us (3%)
    pallas_call x1, Pallas kernels, shards(): pl.pallas_call(kernel, out_shape=jax.ShapeDtypeStruct((2, 8, 2, PART, 2 *...  81.8 us
    unnamed x5, local copies, waits for them, and re-layouts  2.52 us

profile of v4, /device:TPU:1, one launch (start us, length us, event | category | flops | bytes accessed | tf_op | source)
XLA Modules:
  0.0 84.3 jit_solution(9014988499823606543)
XLA Ops:
  0.0 0.0 copy-start.1
  0.0 0.7 copy-done.1
  0.7 0.0 copy-start
  0.7 1.0 %copy-done = bf16[512,512]{1,0:T(8,128)(2,1)S(1)} copy-done((bf16[512,512]{1,0:T(8,128)(2,1)S(1)}, bf16[512,512]{1,0:T(8,128)(2,1)}, u32[]{:S(2)}) %copy-start) | copy-done | bytes 524312
  1.7 81.8 %purify.1 = bf16[2,8,2,16,512]{4,3,2,1,0:T(8,128)(2,1)S(1)} custom-call(bf16[2,256,512]{2,1,0:T(8,128)(2,1)S(1)} %bitcast.3, s32[2,2]{1,0:T(2,128)S(1)} %copy-done.1), custom_call_target="tpu_custom_call" | custom-call | tf_op jit(solution)/shard_map/purify/pallas_call | solution.py:501
  83.5 0.8 copy.4
Async XLA Ops:
  0.0 0.7 copy-start.1
  0.7 1.0 %copy-start = (bf16[512,512]{1,0:T(8,128)(2,1)S(1)}, bf16[512,512]{1,0:T(8,128)(2,1)}, u32[]{:S(2)}) copy-start(bf16[512,512]{1,0:T(8,128)(2,1)} %param.2) | copy-start | bytes 1572868

commit v5 on v4

--- a/solution.py
+++ b/solution.py
@@ -252,6 +252,8 @@
     def column_last(j):
         for da in order:
             column_wait(j, unit(j, da, 2), None, 12 + order[da])
+
+    def share_panel(j):
         ref = pl.ds(0, SLOTS)
         send(cpanel[j].at[:, ref], cpanel[2 + j].at[:, ref], share_send.at[j], share_recv.at[j], mate)
 
@@ -384,49 +386,49 @@
         cube_rows(i, (3, -3, 4))
 
     ring_start(0, 0)
-    column_start()
     ring_start(0, 1)
     ring_start(0, 2)
-    column_near(0, 1)
-    column_near(0, -1)
     ring_hop(0, 0, 1)
-    column_near(1, 1)
-    column_near(1, -1)
+    column_start()
     ring_hop(0, 1, 1)
     ring_start(0, 3)
     ring_hop(0, 2, 1)
+    ring_hop(0, 0, 2)
+    column_near(0, 1)
+    ring_hop(0, 1, 2)
+    column_near(0, -1)
+    ring_hop(0, 3, 1)
+    column_near(1, 1)
+    column_near(1, -1)
+    ring_hop(0, 2, 2)
     column_second(1, 0, 1)
-    ring_hop(0, 0, 2)
+    ring_hop(0, 0, 3)
     column_second(1, 0, -1)
     column_second(0, 0, 1)
     column_second(0, 0, -1)
-    ring_hop(0, 1, 2)
+    ring_hop(0, 1, 3)
     column_far(0)
     column_second(0, -1, 1)
-    ring_hop(0, 3, 1)
+    ring_hop(0, 3, 2)
     column_second(0, -1, -1)
+    ring_hop(0, 2, 3)
+    ring_last(0, 0)
     column_second(1, -1, 1)
     column_second(1, -1, -1)
+    ring_last(0, 1)
     column_second(0, 1, 1)
-    ring_hop(0, 2, 2)
     column_second(0, 1, -1)
+    column_far(1)
     column_second(1, 1, 1)
     column_second(1, 1, -1)
-    ring_hop(0, 0, 3)
-    column_far(1)
-    ring_hop(0, 1, 3)
-    column_second(0, 2, -1)
-    ring_hop(0, 3, 2)
-    ring_hop(0, 2, 3)
-    ring_last(0, 0)
-    column_second(0, 2, 1)
-    ring_last(0, 1)
     ring_hop(0, 3, 3)
     ring_last(0, 2)
-    column_second(1, 2, 1)
+    column_second(0, 2, -1)
+    column_second(0, 2, 1)
+    ring_last(0, 3)
     column_second(1, 2, -1)
     column_last(0)
-    ring_last(0, 3)
+    column_second(1, 2, 1)
     column_last(1)
     gather_rhs(0, 0)
     square(0)
@@ -434,6 +436,8 @@
     gather_rhs(1, 0)
     square(2)
     square(3)
+    share_panel(0)
+    share_panel(1)
     ring_start(1, 0)
     ring_start(1, 1)
     shared_panels()

time: 84.5 us -> 84.6 us (level)
  no operation moved by 1% of the time
where the time goes in v5:
time: 84.6 us; the launch traced here: 84.4 us
  Pallas kernels  81.9 us (97%)
  local copies, waits for them, and re-layouts  2.52 us (3%)
    pallas_call x1, Pallas kernels, shards(): pl.pallas_call(kernel, out_shape=jax.ShapeDtypeStruct((2, 8, 2, PART, 2 *...  81.9 us
    unnamed x5, local copies, waits for them, and re-layouts  2.52 us

profile of v5, /device:TPU:1, one launch (start us, length us, event | category | flops | bytes accessed | tf_op | source)
XLA Modules:
  0.0 84.4 jit_solution(8495248047948035409)
XLA Ops:
  0.0 0.0 copy-start.1
  0.0 0.7 copy-done.1
  0.7 0.0 copy-start
  0.7 1.0 %copy-done = bf16[512,512]{1,0:T(8,128)(2,1)S(1)} copy-done((bf16[512,512]{1,0:T(8,128)(2,1)S(1)}, bf16[512,512]{1,0:T(8,128)(2,1)}, u32[]{:S(2)}) %copy-start) | copy-done | bytes 524312
  1.7 81.9 %purify.1 = bf16[2,8,2,16,512]{4,3,2,1,0:T(8,128)(2,1)S(1)} custom-call(bf16[2,256,512]{2,1,0:T(8,128)(2,1)S(1)} %bitcast.3, s32[2,2]{1,0:T(2,128)S(1)} %copy-done.1), custom_call_target="tpu_custom_call" | custom-call | tf_op jit(solution)/shard_map/purify/pallas_call | solution.py:505
  83.6 0.8 copy.4
Async XLA Ops:
  0.0 0.7 copy-start.1
  0.7 1.0 %copy-start = (bf16[512,512]{1,0:T(8,128)(2,1)S(1)}, bf16[512,512]{1,0:T(8,128)(2,1)}, u32[]{:S(2)}) copy-start(bf16[512,512]{1,0:T(8,128)(2,1)} %param.2) | copy-start | bytes 1572868

commit v6 on v4

--- a/solution.py
+++ b/solution.py
@@ -252,6 +252,8 @@
     def column_last(j):
         for da in order:
             column_wait(j, unit(j, da, 2), None, 12 + order[da])
+
+    def share_panel(j):
         ref = pl.ds(0, SLOTS)
         send(cpanel[j].at[:, ref], cpanel[2 + j].at[:, ref], share_send.at[j], share_recv.at[j], mate)
 
@@ -434,6 +436,8 @@
     gather_rhs(1, 0)
     square(2)
     square(3)
+    share_panel(0)
+    share_panel(1)
     ring_start(1, 0)
     ring_start(1, 1)
     shared_panels()

time: 84.5 us -> 84.4 us (level)
  no operation moved by 1% of the time
where the time goes in v6:
time: 84.4 us; the launch traced here: 84.3 us
  Pallas kernels  81.8 us (97%)
  local copies, waits for them, and re-layouts  2.52 us (3%)
    pallas_call x1, Pallas kernels, shards(): pl.pallas_call(kernel, out_shape=jax.ShapeDtypeStruct((2, 8, 2, PART, 2 *...  81.8 us
    unnamed x5, local copies, waits for them, and re-layouts  2.52 us

profile of v6, /device:TPU:1, one launch (start us, length us, event | category | flops | bytes accessed | tf_op | source)
XLA Modules:
  0.0 84.3 jit_solution(13736852903383256943)
XLA Ops:
  0.0 0.0 copy-start.1
  0.0 0.7 copy-done.1
  0.7 0.0 copy-start
  0.7 1.0 %copy-done = bf16[512,512]{1,0:T(8,128)(2,1)S(1)} copy-done((bf16[512,512]{1,0:T(8,128)(2,1)S(1)}, bf16[512,512]{1,0:T(8,128)(2,1)}, u32[]{:S(2)}) %copy-start) | copy-done | bytes 524312
  1.7 81.8 %purify.1 = bf16[2,8,2,16,512]{4,3,2,1,0:T(8,128)(2,1)S(1)} custom-call(bf16[2,256,512]{2,1,0:T(8,128)(2,1)S(1)} %bitcast.3, s32[2,2]{1,0:T(2,128)S(1)} %copy-done.1), custom_call_target="tpu_custom_call" | custom-call | tf_op jit(solution)/shard_map/purify/pallas_call | solution.py:505
  83.5 0.8 copy.4
Async XLA Ops:
  0.0 0.7 copy-start.1
  0.7 1.0 %copy-start = (bf16[512,512]{1,0:T(8,128)(2,1)S(1)}, bf16[512,512]{1,0:T(8,128)(2,1)}, u32[]{:S(2)}) copy-start(bf16[512,512]{1,0:T(8,128)(2,1)} %param.2) | copy-start | bytes 1572868
